TPU v7x, 32 devices: a whole 2x2x4 slice. The times are simulated.
32 devices in a mesh: dp: 8 (over z, x), tensor: 4 (over y, core).
Axes of the slice: x: 2, y: 2, z: 4, core: 2. Of those that a mesh axis runs over, the one named last changes fastest.
Arguments:
- tokens: bfloat16 [8192, 2048], P(('dp', 'tensor')), may hold values from -6 to 6
- gain_attn: float32 [2048], replicated, may hold values from 0.5 to 1.5
- gain_mlp: float32 [2048], replicated, may hold values from 0.5 to 1.5
- w_query: bfloat16 [2048, 256], P(None, 'tensor'), may hold values from -0.125 to 0.125
- w_key: bfloat16 [2048, 256], P(None, 'tensor'), may hold values from -0.125 to 0.125
- w_value: bfloat16 [2048, 2048], P(None, 'tensor'), may hold values from -0.125 to 0.125
- w_out: bfloat16 [2048, 2048], P('tensor'), may hold values from -1.5 to 1.5
- w_gate: bfloat16 [2048, 5504], P(None, 'tensor'), may hold values from -0.125 to 0.125
- w_up: bfloat16 [2048, 5504], P(None, 'tensor'), may hold values from -0.125 to 0.125
- w_down: bfloat16 [5504, 2048], P('tensor'), may hold values from -0.078125 to 0.078125
- cotangent: bfloat16 [8192, 2048], P(('dp', 'tensor')), may hold values from -6 to 6
- lengths: int32 [8], replicated, may hold values from 256 to 1024, as said below
Outputs:
- output: bfloat16 [8192, 2048], P(('dp', 'tensor'))
- input_grad: float32 [8192, 2048], P(('dp', 'tensor'))
- gain_attn_grad: float32 [2048], replicated
- gain_mlp_grad: float32 [2048], replicated
- query_grad: float32 [2048, 256], P('dp', 'tensor')
- key_grad: float32 [2048, 256], P('dp', 'tensor')
- value_grad: float32 [2048, 2048], P('dp', 'tensor')
- out_grad: float32 [2048, 2048], P('tensor', 'dp')
- gate_grad: float32 [2048, 5504], P('dp', 'tensor')
- up_grad: float32 [2048, 5504], P('dp', 'tensor')
- down_grad: float32 [5504, 2048], P('tensor', 'dp')
- den_mean: float32 [], replicated
Inputs may be any that keep to these rules, and one draw needn't show every extreme that they name: `lengths`: some sequence has length exactly 1024 and some other exactly 256.
All inputs are finite; a program needn't handle non-finite values.
Results may differ from a plain program's by a relative error of at most 0.018.
Values may be sent and summed in bfloat16 or wider, within the bound.
A program may use at most 192 MiB of HBM per device.

v0:
```python
import functools
import math

import jax
import jax.numpy as jnp
from jax import lax
from jax.experimental import pallas as pl
from jax.experimental.pallas import tpu as pltpu
from jax.sharding import PartitionSpec as P

FEAT = 16
MESH = pl.DeviceIdType.MESH
f32 = jnp.float32
bf16 = jnp.bfloat16
NT = (((1,), (1,)), ((), ()))
TN = (((0,), (0,)), ((), ()))
AHEAD = 4
LAG = 2
SETTLE = 3
STRIP = 16


def dot(a, b, dims=(((1,), (0,)), ((), ()))):
    return lax.dot_general(a, b, dims, preferred_element_type=f32)


def loop(count, body):
    def step(i, carry):
        body(i)
        return carry

    lax.fori_loop(0, count, step, 0)


def pieces(width, size):
    return [(start, min(size, width - start)) for start in range(0, width, size)]


class Group:
    def __init__(self):
        self.dp = lax.axis_index("dp")
        self.t = lax.axis_index("tensor")
        self.y, self.c = self.t // 2, lax.rem(self.t, 2)
        self.sibling = (self.dp, self.y * 2 + 1 - self.c)
        self.across = (self.dp, (1 - self.y) * 2 + self.c)


def remote(src, dst, send, recv, device):
    return pltpu.make_async_remote_copy(src, dst, send, recv, device_id=device, device_id_type=MESH)


class RowSums:
    def __init__(self, g, own_rows, phase, chunk, part, bufs, sems):
        self.g, self.own, self.p, self.chunk, self.part = g, own_rows, phase, chunk, part
        self.sibsend, self.sibrecv, self.ysend, self.yrecv, self.total = bufs
        self.sib_s, self.sib_r, self.y_s, self.y_r = sems
        self.count = own_rows // chunk

    def at(self, j):
        return pl.ds(pl.multiple_of(j * self.chunk, self.chunk), self.chunk)

    def rows(self, y, c, j):
        return pl.ds(pl.multiple_of((y * 2 + c) * self.own + j * self.chunk, self.chunk), self.chunk)

    def sib(self, far, j):
        return remote(
            self.sibsend.at[far, self.at(j)], self.sibrecv.at[far, self.at(j)],
            self.sib_s.at[self.p, far, j], self.sib_r.at[self.p, far, j], self.g.sibling,
        )

    def ycopy(self, j):
        return remote(
            self.ysend.at[self.at(j)], self.yrecv.at[self.at(j)],
            self.y_s.at[self.p, j], self.y_r.at[self.p, j], self.g.across,
        )

    def give(self, far, j):
        y = 1 - self.g.y if far else self.g.y
        for n, w in pieces(self.total.shape[1], 512):
            self.sibsend[far, self.at(j), n : n + w] = self.part(self.rows(y, 1 - self.g.c, j), n, w).astype(bf16)
        self.sib(far, j).start()

    def send(self, j):
        g = self.g
        for n, w in pieces(self.total.shape[1], 512):
            self.total[self.at(j), n : n + w] = self.part(self.rows(1 - g.y, g.c, j), n, w)
        self.sib(1, j).wait_recv()
        self.ysend[self.at(j)] = (self.total[self.at(j)] + self.sibrecv[1, self.at(j)].astype(f32)).astype(bf16)
        self.ycopy(j).start()

    def hold(self, j):
        for n, w in pieces(self.total.shape[1], 512):
            self.total[self.at(j), n : n + w] = self.part(self.rows(self.g.y, self.g.c, j), n, w)

    def finish(self, j, use):
        self.sib(0, j).wait_recv()
        self.ycopy(j).wait_recv()

        def strip(i):
            r = pl.ds(pl.multiple_of(j * self.chunk + i * STRIP, STRIP), STRIP)
            use(r, self.total[r] + self.sibrecv[0, r].astype(f32) + self.yrecv[r].astype(f32))

        loop(self.chunk // STRIP, strip)

    def drain(self):
        def body(j):
            self.sib(0, j).wait_send()
            self.sib(1, j).wait_send()
            self.ycopy(j).wait_send()

        loop(self.count, body)


class Spread:
    def __init__(self, g, own_rows, chunk, src, full, sems, phase):
        self.g, self.own, self.chunk, self.src, self.full, self.p = g, own_rows, chunk, src, full, phase
        self.s, self.r = sems
        self.count = own_rows // chunk

    def rows(self, y, c, j):
        return pl.ds(pl.multiple_of((y * 2 + c) * self.own + j * self.chunk, self.chunk), self.chunk)

    def copy(self, kind, j):
        g = self.g
        rows = self.rows(g.y, g.c, j)
        if kind == 2:
            rows = self.rows(1 - g.y, g.c, j)
            src = self.full.at[rows]
        elif self.src is None:
            src = self.full.at[rows]
        else:
            src = self.src.at[pl.ds(pl.multiple_of(j * self.chunk, self.chunk), self.chunk)]
        return remote(
            src, self.full.at[rows], self.s.at[self.p, kind, j], self.r.at[self.p, kind, j],
            g.across if kind == 1 else g.sibling,
        )

    def start(self, j):
        self.copy(1, j).start()
        self.copy(0, j).start()

    def relay(self, j):
        self.copy(1, j).wait_recv()
        self.copy(2, j).start()

    def sib_in(self, j):
        self.copy(0, j).wait_recv()

    def far_in(self, j):
        self.copy(2, j).wait_recv()

    def drain(self):
        def body(j):
            for kind in range(3):
                self.copy(kind, j).wait_send()

        loop(self.count, body)


class WeightSums:
    def __init__(self, g, dp_size, rows, jobs, z_first, block, refs, sems, emit):
        self.g, self.rows, self.block, self.z_first, self.emit = g, rows, block, z_first, emit
        self.nz = dp_size // 2
        self.z, self.x = g.dp // 2, lax.rem(g.dp, 2)
        self.halves = max(1, rows // 128)
        self.rn = rows // self.halves
        self.ring = self.zs_slots(self.nz)
        self.jobs = jobs * self.halves - z_first
        self.steps = self.jobs * self.nz
        self.xs, self.zs, self.acc, self.xtmp, self.ztmp, self.xrecv, self.zrecv = refs[:7]
        self.xs_s, self.xr_s, self.zs_s, self.zr_s, self.loc = sems[:5]
        if z_first:
            self.zf, self.zfx, self.facc, self.frecv, self.fxrecv = refs[7:]
            self.zf_s, self.zf_r, self.fx_s, self.fx_r = sems[5:]
        self.ahead = self.xs.shape[0]
        self.partner = (self.z * 2 + 1 - self.x, g.t)

    @staticmethod
    def zs_slots(nz):
        return 2 * nz if nz <= 4 else nz

    def job(self, s):
        lin = s // self.nz + self.z_first
        return lin // self.halves, lax.rem(lin, self.halves)

    def order(self, k):
        last = self.nz - 1
        upper = self.z >= self.nz // 2
        z = jnp.where(upper, last - self.z, self.z)
        zt = jnp.where(k < last - z, last - k, jnp.where(k < last, last - 1 - k, z))
        return jnp.where(upper, last - zt, zt)

    def coming(self, zt):
        return jnp.where(zt > self.z, self.z > 0, self.z < self.nz - 1)

    def towards(self, zt):
        return (jnp.where(zt > self.z, self.z + 1, self.z - 1) * 2 + self.x, self.g.t)

    def slot(self, zt):
        return jnp.where(zt == self.z - 1, self.nz, zt)

    def xcopy(self, s):
        slot = lax.rem(s, self.ahead)
        return remote(self.xs.at[slot], self.xrecv.at[s], self.xs_s.at[slot], self.xr_s.at[s], self.partner)

    def zcopy(self, s, zt):
        ring = lax.rem(s, self.ring)
        j = s // self.nz * (self.nz + 1) + self.slot(zt)
        return remote(self.zs.at[ring], self.zrecv.at[j], self.zs_s.at[ring], self.zr_s.at[j], self.towards(zt))

    def zwait(self, j):
        remote(self.zs.at[0], self.zrecv.at[j], self.zs_s.at[0], self.zr_s.at[j], self.partner).wait_recv()

    def fetch(self, src, dst, k):
        copy = pltpu.make_async_copy(src, dst, self.loc.at[k])
        copy.start()
        return copy

    def xsend(self, s):
        @pl.when(s >= self.ahead)
        def _():
            self.xcopy(s - self.ahead).wait_send()

        i, h = self.job(s)
        self.xs[lax.rem(s, self.ahead)] = self.block(i, self.order(lax.rem(s, self.nz)), 1 - self.x, h).astype(bf16)
        self.xcopy(s).start()

    def xstep(self, s):
        k = lax.rem(s, self.nz)
        zt = self.order(k)
        i, h = self.job(s)
        self.xcopy(s).wait_recv()
        copy = self.fetch(self.xrecv.at[s], self.xtmp, 0)
        own = self.block(i, zt, self.x, h)
        slot = lax.rem(s // self.nz, 2)
        ring = lax.rem(s, self.ring)

        @pl.when((s >= self.ring) & (k < self.nz - 1))
        def _():
            self.zcopy(s - self.ring, zt).wait_send()

        self.acc[slot] = own
        copy.wait()
        total = self.acc[slot] + self.xtmp[...].astype(f32)

        @pl.when(k == self.nz - 1)
        def _():
            self.acc[slot] = total

        @pl.when(k < self.nz - 1)
        def _():
            self.zs[ring] = total.astype(bf16)

            @pl.when(jnp.logical_not(self.coming(zt)))
            def _():
                self.zcopy(s, zt).start()

    def zstep(self, s):
        k = lax.rem(s, self.nz)
        zt = self.order(k)
        ring = lax.rem(s, self.ring)

        @pl.when((k < self.nz - 1) & self.coming(zt))
        def _():
            j = s // self.nz * (self.nz + 1) + zt
            self.zwait(j)
            self.fetch(self.zrecv.at[j], self.ztmp.at[pl.ds(0, self.rn)], 1).wait()
            self.zs[ring] = (self.zs[ring].astype(f32) + self.ztmp[: self.rn].astype(f32)).astype(bf16)
            self.zcopy(s, zt).start()

    def final(self, jx):
        slot = lax.rem(jx, 2)

        def take(j):
            self.zwait(j)
            self.fetch(self.zrecv.at[j], self.ztmp.at[pl.ds(0, self.rn)], 1).wait()
            self.acc[slot] += self.ztmp[: self.rn].astype(f32)

        @pl.when(self.z > 0)
        def _():
            take(jx * (self.nz + 1) + self.z)

        @pl.when(self.z < self.nz - 1)
        def _():
            take(jx * (self.nz + 1) + self.nz)

        i, h = self.job(jx * self.nz)
        self.emit(i, h, lambda n, w: self.acc[slot, :, n : n + w])

    def fcopy(self, q, zt):
        slot = self.slot(zt)
        return remote(self.zf.at[q], self.frecv.at[slot], self.zf_s.at[q], self.zf_r.at[slot], self.towards(zt))

    def fwait(self, slot):
        remote(self.zf.at[0], self.frecv.at[slot], self.zf_s.at[0], self.zf_r.at[slot], self.partner).wait_recv()

    def fstart(self, q):
        zt = self.order(q)
        for xt in range(2):
            self.zf[q, xt * self.rn : (xt + 1) * self.rn] = self.block(0, zt, xt, 0).astype(bf16)

        @pl.when(jnp.logical_not(self.coming(zt)))
        def _():
            self.fcopy(q, zt).start()

    def fstep(self, q):
        zt = self.order(q)

        @pl.when(self.coming(zt))
        def _():
            self.fwait(zt)
            self.fetch(self.frecv.at[zt], self.ztmp, 1).wait()
            self.zf[q] = (self.zf[q].astype(f32) + self.ztmp[...].astype(f32)).astype(bf16)
            self.fcopy(q, zt).start()

    def fxcopy(self):
        return remote(self.zfx, self.fxrecv, self.fx_s.at[0], self.fx_r.at[0], self.partner)

    def fend(self):
        for xt in range(2):
            self.facc[xt * self.rn : (xt + 1) * self.rn] = self.block(0, self.z, xt, 0)

        def take(slot):
            self.fwait(slot)
            self.fetch(self.frecv.at[slot], self.ztmp, 1).wait()
            self.facc[...] += self.ztmp[...].astype(f32)

        @pl.when(self.z > 0)
        def _():
            take(self.z)

        @pl.when(self.z < self.nz - 1)
        def _():
            take(self.nz)

        away = pl.ds(pl.multiple_of((1 - self.x) * self.rn, self.rn), self.rn)
        self.zfx[...] = self.facc[away].astype(bf16)
        self.fxcopy().start()

    def ffinal(self):
        self.fxcopy().wait_recv()
        self.fetch(self.fxrecv, self.xtmp, 1).wait()
        own = pl.ds(pl.multiple_of(self.x * self.rn, self.rn), self.rn)
        self.facc[own] += self.xtmp[...].astype(f32)
        self.emit(0, 0, lambda n, w: self.facc[own, n : n + w])

    def begin(self):
        loop(self.ahead, self.xsend)
        if self.z_first:
            loop(self.nz - 1, self.fstart)

    def services(self):
        return max(self.steps + SETTLE + 1, self.z_first * (2 * self.nz + 5))

    def service(self, s):
        @pl.when(s < self.steps)
        def _():
            self.xstep(s)

        @pl.when(s + self.ahead < self.steps)
        def _():
            self.xsend(s + self.ahead)

        @pl.when((s >= LAG) & (s - LAG < self.steps))
        def _():
            self.zstep(s - LAG)

        if self.z_first:

            @pl.when((lax.rem(s, 2) == 1) & (s // 2 < self.nz - 1))
            def _():
                self.fstep(s // 2)

            @pl.when(s == 2 * self.nz - 1)
            def _():
                self.fend()

            @pl.when(s == 2 * self.nz + 4)
            def _():
                self.ffinal()

        @pl.when((s >= self.nz + SETTLE) & (lax.rem(s - SETTLE, self.nz) == 0) & (s - SETTLE <= self.steps))
        def _():
            self.final((s - SETTLE) // self.nz - 1)

    def drain(self):
        loop(self.ahead, lambda a: self.xcopy(self.steps - self.ahead + a).wait_send())

        def zdone(a):
            s = self.steps - self.ring + a
            k = lax.rem(s, self.nz)

            @pl.when(k < self.nz - 1)
            def _():
                self.zcopy(s, self.order(k)).wait_send()

        loop(self.ring, zdone)
        if self.z_first:
            loop(self.nz - 1, lambda q: self.fcopy(q, self.order(q)).wait_send())
            self.fxcopy().wait_send()


def meet(g, nz, every=False):
    z, x = g.dp // 2, lax.rem(g.dp, 2)
    barrier = pltpu.get_barrier_semaphore()

    def hello(device):
        pl.semaphore_signal(barrier, inc=1, device_id=device, device_id_type=MESH)

    hello(g.sibling)
    hello(g.across)
    hello((z * 2 + 1 - x, g.t))
    if every:
        loop(nz - 1, lambda k: hello((lax.rem(z + 1 + k, nz) * 2 + x, g.t)))
        pl.semaphore_wait(barrier, nz + 2)
        return

    @pl.when(z > 0)
    def _():
        hello(((z - 1) * 2 + x, g.t))

    @pl.when(z < nz - 1)
    def _():
        hello(((z + 1) * 2 + x, g.t))

    peers = 5 - jnp.where(z == 0, 1, 0) - jnp.where(z == nz - 1, 1, 0)
    pl.semaphore_wait(barrier, peers)


def turned(out, turn, sem, halves, rn):
    def emit(i, h, value):
        for n, w in pieces(out.shape[1], 512):
            turn[:w] = value(n, w).T
            to = out.at[i, pl.ds(n, w)]
            if halves > 1:
                to = out.at[i, pl.ds(n, w), pl.ds(pl.multiple_of(h * rn, rn), rn)]
            copy = pltpu.make_async_copy(turn.at[pl.ds(0, w)], to, sem)
            copy.start()
            copy.wait()

    return emit


def block_of(lefts, rights, left_of, rows, halves):
    rn = rows // halves

    def block(i, zt, xt, h):
        li, right = left_of(i), rights.at[i]
        if rows % 128:
            cols = pl.ds(pl.multiple_of(zt * (2 * rows), 2 * rows), 2 * rows)
            both = dot(lefts[li, :, cols], right[...], TN)
            return jnp.where(xt == 0, both[:rows], both[rows:])
        cols = pl.ds(pl.multiple_of((zt * 2 + xt) * rows + h * rn, rn), rn)
        return dot(lefts[li, :, cols], right[...], TN)

    return block


def norm_parts(state):
    scale = lax.rsqrt(jnp.mean(state * state, axis=-1, keepdims=True) + 1e-06)
    return state * scale, scale


def mlp_kernel(
    dp_size,
    attended, w_out, gain, valid, tokens_h, w_gate_h, w_up_h, w_down_h, cot_h,
    output, state_grad_h, gain_grad, state_all_h, totals_h, xrecv, zrecv, frecv, fxrecv,
    w_gate, w_up, w_down, lefts, rights, mid, sibsend, sibrecv, ysend, yrecv, total, spread_buf,
    xs, zs, zf, zfx, acc, facc, xtmp, ztmp, turn,
    load_sem, sib_s, sib_r, y_s, y_r, ag_s, ag_r,
    xs_s, xr_s, zs_s, zr_s, zf_s, zf_r, fx_s, fx_r, loc,
):
    g = Group()
    own_rows, width = tokens_h.shape
    tokens = spread_buf
    hidden_units = rights.shape[2]
    rows = width // dp_size
    loads = [
        pltpu.make_async_copy(src, dst, load_sem.at[n])
        for n, (src, dst) in enumerate(
            [(w_gate_h, w_gate), (w_up_h, w_up), (w_down_h, w_down), (cot_h, lefts.at[0]), (tokens_h, tokens)]
        )
    ]
    for copy in loads:
        copy.start()
    meet(g, dp_size // 2)
    bufs = (sibsend, sibrecv, ysend, yrecv, total)
    sems = (sib_s, sib_r, y_s, y_r)

    def attn_part(r, n, w):
        return dot(attended[r], w_out[:, n : n + w])

    sums = RowSums(g, own_rows, 0, 64, attn_part, bufs, sems)
    normed = Spread(g, own_rows, 64, None, lefts.at[1], (ag_s, ag_r), 0)
    own_first = pl.multiple_of(g.t * own_rows, own_rows)

    def first_state(r, summed):
        state = tokens[r].astype(f32) + summed
        mid[r] = state
        normal, _ = norm_parts(state)
        start = pl.multiple_of(own_first + r.start, STRIP)
        lefts[1, pl.ds(start, STRIP)] = (normal * gain[...]).astype(bf16)

    sums.give(1, 0)

    def far(j):
        @pl.when(j + 1 < sums.count)
        def _():
            sums.give(1, j + 1)

        sums.send(j)

    loop(sums.count, far)

    def near(j):
        sums.give(0, j)
        sums.hold(j)

    loop(sums.count, near)

    def feed(y, c, half):
        r = pl.ds(pl.multiple_of((y * 2 + c) * own_rows + half * 128, 128), 128)
        for n, w in pieces(hidden_units, 512):
            gate = dot(lefts[1, r], w_gate[n : n + w], NT)
            up = dot(lefts[1, r], w_up[n : n + w], NT)
            back = dot(lefts[0, r], w_down[n : n + w], NT)
            sig = jax.nn.sigmoid(gate)
            active = gate * sig
            rights[0, r, n : n + w] = (active * up).astype(bf16)
            rights[1, r, n : n + w] = (back * up * sig * (1.0 + gate * (1.0 - sig))).astype(bf16)
            rights[2, r, n : n + w] = (back * active).astype(bf16)

    def close(j):
        sums.finish(j, first_state)
        normed.start(j)

    loads[4].wait()

    def half_near(half):
        loop(2, lambda a: close(half * 2 + a))

        @pl.when(half == 0)
        def _():
            for copy in loads[:4]:
                copy.wait()

        feed(g.y, g.c, half)
        loop(2, lambda a: normed.sib_in(half * 2 + a))
        feed(g.y, 1 - g.c, half)

    loop(2, half_near)

    def half_far(half):
        loop(2, lambda a: normed.relay(half * 2 + a))
        feed(1 - g.y, g.c, half)
        loop(2, lambda a: normed.far_in(half * 2 + a))
        feed(1 - g.y, 1 - g.c, half)

    loop(2, half_far)
    sums.drain()

    halves = max(1, rows // 128)
    rn = rows // halves
    engine = WeightSums(
        g, dp_size, rows, 3, 1, block_of(lefts, rights, lambda i: jnp.minimum(i, 1), rows, halves),
        (xs, zs, acc, xtmp, ztmp, xrecv, zrecv, zf, zfx, facc, frecv, fxrecv),
        (xs_s, xr_s, zs_s, zr_s, loc, zf_s, zf_r, fx_s, fx_r), turned(totals_h, turn, loc.at[2], halves, rn),
    )
    engine.begin()

    def back_part(r, n, w):
        return dot(rights[1, r], w_gate[:, n : n + w]) + dot(rights[2, r], w_up[:, n : n + w])

    sums = RowSums(g, own_rows, 1, 128, back_part, bufs, sems)
    states = Spread(g, own_rows, 128, spread_buf, state_all_h, (ag_s, ag_r), 1)
    gain_grad[...] = jnp.zeros_like(gain_grad)

    def state_back(r, grad):
        normal, scale = norm_parts(mid[r])
        weighted = grad * gain[...]
        start = pl.multiple_of(own_first + r.start, STRIP)
        change = scale * (weighted - normal * jnp.mean(weighted * normal, axis=-1, keepdims=True))
        state = lefts[0, pl.ds(start, STRIP)].astype(f32) + change
        gain_grad[...] += jnp.sum(grad * normal, axis=0, keepdims=True)
        total[r] = state
        spread_buf[r] = state.astype(bf16)

    def far_back(j):
        sums.give(1, j)
        sums.send(j)

    loop(sums.count, far_back)

    def near_back(j):
        sums.give(0, j)
        engine.service(2 * j)
        sums.hold(j)
        engine.service(2 * j + 1)

    loop(sums.count, near_back)
    used = 2 * sums.count

    def own_copy(j):
        r = pl.ds(pl.multiple_of(j * 128, 128), 128)
        to = pl.ds(pl.multiple_of(own_first + j * 128, 128), 128)
        return (
            pltpu.make_async_copy(total.at[r], state_grad_h.at[r], load_sem.at[0]),
            pltpu.make_async_copy(spread_buf.at[r], state_all_h.at[to], load_sem.at[1]),
        )

    def close_back(j):
        sums.finish(j, state_back)
        states.start(j)
        copies = own_copy(j)
        for copy in copies:
            copy.start()
        engine.service(used + j)
        for copy in copies:
            copy.wait()

    loop(sums.count, close_back)
    used = used + sums.count

    def pass_back(j):
        states.relay(j)
        engine.service(used + j)

    loop(sums.count, pass_back)
    used = used + sums.count

    def arrive(j):
        states.sib_in(j)
        states.far_in(j)

    loop(sums.count, arrive)
    sums.drain()

    def down_part(r, n, w):
        return dot(rights[0, r], w_down[:, n : n + w])

    sums = RowSums(g, own_rows, 2, 128, down_part, bufs, sems)

    def far_down(j):
        sums.give(1, j)
        engine.service(used + 2 * j)
        sums.send(j)
        engine.service(used + 2 * j + 1)

    loop(sums.count, far_down)
    used = used + 2 * sums.count

    def near_down(j):
        sums.give(0, j)
        sums.hold(j)
        engine.service(used + j)

    loop(sums.count, near_down)
    used = used + sums.count

    def last_state(r, summed):
        output[r] = (valid[r] * (mid[r] + summed)).astype(bf16)

    loop(sums.count, lambda j: sums.finish(j, last_state))
    loop(engine.services() - used, lambda n: engine.service(used + n))
    sums.drain()
    normed.drain()
    states.drain()
    engine.drain()


def mlp_call(attended, w_out, tokens, gain, valid, w_gate, w_up, w_down, cot_all, collective_id):
    dp_size = lax.axis_size("dp")
    nz = dp_size // 2
    own_rows, width = tokens.shape
    bucket = cot_all.shape[0]
    units = w_down.shape[0]
    rows = width // dp_size
    halves = max(1, rows // 128)
    rn = rows // halves
    jobs = 3 * halves - 1
    steps = jobs * nz
    vm, hbm = pl.BlockSpec(memory_space=pltpu.VMEM), pl.BlockSpec(memory_space=pl.ANY)
    dma = lambda *shape: pltpu.SemaphoreType.DMA(shape)
    vmem = lambda shape, kind=bf16: pltpu.VMEM(shape, kind)
    sds = jax.ShapeDtypeStruct
    outs = pl.pallas_call(
        functools.partial(mlp_kernel, dp_size),
        out_shape=[
            sds((own_rows, width), bf16),
            sds((own_rows, width), f32),
            sds((1, width), f32),
            sds((bucket, width), bf16),
            sds((3, units, rows), f32),
            sds((steps, rn, units), bf16),
            sds((jobs * (nz + 1), rn, units), bf16),
            sds((nz + 1, 2 * rn, units), bf16),
            sds((rn, units), bf16),
        ],
        in_specs=[vm] * 4 + [hbm] * 5,
        out_specs=[vm, hbm, vm] + [hbm] * 6,
        scratch_shapes=[
            vmem((units, width)), vmem((units, width)), vmem((units, width)),
            vmem((2, bucket, width)), vmem((3, bucket, units)), vmem((own_rows, width), f32),
            vmem((2, own_rows, width)), vmem((2, own_rows, width)), vmem((own_rows, width)), vmem((own_rows, width)),
            vmem((own_rows, width), f32), vmem((own_rows, width)),
            vmem((AHEAD, rn, units)), vmem((WeightSums.zs_slots(nz), rn, units)), vmem((nz - 1, 2 * rn, units)), vmem((rn, units)),
            vmem((2, rn, units), f32), vmem((2 * rn, units), f32), vmem((rn, units)), vmem((2 * rn, units)),
            vmem((512, rn), f32),
            dma(5), dma(3, 2, 4), dma(3, 2, 4), dma(3, 4), dma(3, 4), dma(2, 3, 4), dma(2, 3, 4),
            dma(AHEAD), dma(steps), dma(WeightSums.zs_slots(nz)), dma(jobs * (nz + 1)), dma(nz), dma(nz + 1), dma(1), dma(1), dma(3),
        ],
        compiler_params=pltpu.CompilerParams(
            collective_id=collective_id, has_side_effects=True, vmem_limit_bytes=62 << 20
        ),
        name="mlp",
    )(attended, w_out, gain, valid, tokens, w_gate, w_up, w_down, cot_all)
    return outs[:5]


def head_lanes(h, feat, width):
    return (lax.broadcasted_iota(jnp.int32, (1, width), 1) // feat == h).astype(f32).astype(bf16)


def back_kernel(
    dp_size,
    state_all, attended, w_out, numer, denom, key_valid, query, key, value, gain, small_in,
    normed_h, w_query_h, w_key_h, w_value_h, tokens_h, grad_state_h,
    small_out, input_grad_h, out_h, value_h, qk_h, xrecv_o, zrecv_o, xrecv_a, zrecv_a,
    normed, w_query, w_key, w_value, tokens, grad_state, grad_numer, grad_den, key_t, rights,
    gv_acc, gk_acc, gq_acc, sibsend, sibrecv, ysend, yrecv, total,
    xs_o, zs_o, acc_o, xtmp_o, ztmp_o, xs_a, zs_a, acc_a, xtmp_a, ztmp_a, turn, gain_acc, smalls, small_got, small_z,
    load_sem, sib_s, sib_r, y_s, y_r,
    xs_so, xr_so, zs_so, zr_so, loc_o, xs_sa, xr_sa, zs_sa, zr_sa, loc_a, sm_s, sm_r, smz_s, smz_r,
):
    g = Group()
    nz = dp_size // 2
    own_rows, width = tokens_h.shape
    bucket = state_all.shape[1]
    head_width = 128
    feat_width = query.shape[1]
    heads = attended.shape[2] // head_width
    feat = feat_width // heads
    rows = width // dp_size
    halves = max(1, rows // 128)
    rn = rows // halves
    scale = 1.0 / math.sqrt(feat)
    loads = [
        pltpu.make_async_copy(src, dst, load_sem.at[n])
        for n, (src, dst) in enumerate(
            [
                (normed_h, normed.at[0]), (w_query_h, w_query), (w_key_h, w_key), (w_value_h, w_value),
                (tokens_h, tokens), (grad_state_h, grad_state),
            ]
        )
    ]
    for copy in loads:
        copy.start()
    meet(g, nz, every=True)

    first = WeightSums(
        g, dp_size, rows, 1, 0, block_of(state_all, attended, lambda i: i, rows, halves),
        (xs_o, zs_o, acc_o, xtmp_o, ztmp_o, xrecv_o, zrecv_o),
        (xs_so, xr_so, zs_so, zr_so, loc_o), turned(out_h, turn, loc_o.at[2], halves, rn),
    )
    turn_qk = turned(qk_h, turn, loc_a.at[2], halves, rn)

    def emit_attn(i, h, take):
        values = heads * head_width
        copy = pltpu.make_async_copy(
            total.at[pl.ds(0, rn), pl.ds(0, values)], value_h.at[pl.ds(pl.multiple_of(h * rn, rn), rn)], loc_a.at[2]
        )
        total[:rn, :values] = take(0, values)
        copy.start()
        copy.wait()
        turn_qk(i, h, lambda n, w: take(values + n, w))

    second = WeightSums(
        g, dp_size, rows, 1, 0, block_of(normed, rights, lambda i: i, rows, halves),
        (xs_a, zs_a, acc_a, xtmp_a, ztmp_a, xrecv_a, zrecv_a),
        (xs_sa, xr_sa, zs_sa, zr_sa, loc_a), emit_attn,
    )
    first.begin()
    key_t[...] = key[...].astype(f32).T.astype(bf16)

    def spread_grad(b):
        r = pl.ds(pl.multiple_of(b * 128, 128), 128)
        grad = dot(state_all[0, r], w_out[...], NT).astype(bf16).astype(f32)
        lane = lax.broadcasted_iota(jnp.int32, (128, 128), 1)
        dens = jnp.zeros((128, 128), f32)
        for h in range(heads):
            cols = slice(h * head_width, (h + 1) * head_width)
            den = denom[r, h : h + 1]
            part = grad[:, cols]
            grad_numer[r, cols] = (part / den).astype(bf16)
            back = -jnp.sum(part * numer[r, cols], axis=1, keepdims=True) / (den * den)
            dens = jnp.where(lane == h, back, dens)
        grad_den[:, r] = dens.T[: grad_den.shape[0]]

    loop(bucket // 128, spread_grad)
    gk_acc[...] = jnp.zeros_like(gk_acc)
    gq_acc[...] = jnp.zeros_like(gq_acc)
    gv_acc[...] = jnp.zeros_like(gv_acc)
    tile = 256

    def head(h):
        lanes = head_lanes(h, feat, feat_width)
        cols = pl.ds(pl.multiple_of(h * head_width, head_width), head_width)
        sub = lax.broadcasted_iota(jnp.int32, (feat_width, 1), 0) // feat == h
        for qb in range(bucket // tile):
            q0, nk = qb * tile, (qb + 1) * tile
            q_own = query[q0:nk] * lanes
            kept = key_t[:, :nk] * sub.astype(f32).astype(bf16)
            scores = dot(key[:nk], q_own, NT) * scale
            below = lax.broadcasted_iota(jnp.int32, (nk, tile), 0) <= q0 + lax.broadcasted_iota(
                jnp.int32, (nk, tile), 1
            )
            mask = below.astype(f32) * key_valid[:nk]
            taylor = (1.0 + scores + 0.5 * scores * scores) * mask
            grads = grad_numer[q0:nk, cols]
            gv_acc[:nk, cols] += dot(taylor.astype(bf16), grads)
            back = dot(value[:nk, cols], grads, NT) + grad_den[pl.ds(h, 1), q0:nk]
            low = (back * mask * (1.0 + scores)).astype(bf16)
            gk_acc[:nk] += dot(low, q_own)
            gq_acc[:, q0:nk] += dot(kept, low)
        first.service(2 * h)
        first.service(2 * h + 1)

    loop(heads, head)
    used = 2 * heads
    values = heads * head_width
    rights[0, :, :values] = gv_acc[...].astype(bf16)
    rights[0, :, values:] = jnp.concatenate([gq_acc[...].T * scale, gk_acc[...] * scale], axis=1).astype(bf16)
    for copy in loads:
        copy.wait()
    second.begin()

    def part(r, n, w):
        out = dot(rights[0, r, :values], w_value[n : n + w], NT)
        out = out + dot(rights[0, r, values : values + feat_width], w_query[:, n : n + w])
        return out + dot(rights[0, r, values + feat_width :], w_key[:, n : n + w])

    sums = RowSums(g, own_rows, 0, 128, part, (sibsend, sibrecv, ysend, yrecv, total), (sib_s, sib_r, y_s, y_r))

    def far(j):
        sums.give(1, j)
        first.service(used + 2 * j)
        sums.send(j)
        first.service(used + 2 * j + 1)

    loop(sums.count, far)
    used = used + 2 * sums.count

    def near(j):
        sums.give(0, j)
        second.service(2 * j)
        sums.hold(j)
        second.service(2 * j + 1)

    loop(sums.count, near)
    gain_acc[...] = jnp.zeros_like(gain_acc)

    def last(r, grad):
        normal, inv = norm_parts(tokens[r].astype(f32))
        weighted = grad * gain[...]
        change = inv * (weighted - normal * jnp.mean(weighted * normal, axis=-1, keepdims=True))
        gain_acc[...] += jnp.sum(grad * normal, axis=0, keepdims=True)
        grad_state[r] += change

    def close(j):
        sums.finish(j, last)
        r = pl.ds(pl.multiple_of(j * sums.chunk, sums.chunk), sums.chunk)
        pltpu.make_async_copy(grad_state.at[r], input_grad_h.at[r], load_sem.at[0]).start()
        second.service(2 * sums.count + j)
        pltpu.make_async_copy(grad_state.at[r], input_grad_h.at[r], load_sem.at[0]).wait()

    loop(sums.count, close)
    done = 3 * sums.count

    smalls[0] = small_in[...]
    smalls[0, 0:1] = gain_acc[...]
    z, x = second.z, second.x
    peers = (g.sibling, g.across, second.partner)
    for n, device in enumerate(peers):
        copy = remote(smalls.at[n], small_got.at[n], sm_s.at[n], sm_r.at[n], device)
        copy.start()
        second.service(done + n)
        copy.wait()
        smalls[n + 1] = smalls[n] + small_got[n]
    done = done + len(peers)

    def zsmall(k):
        return remote(
            smalls.at[3], small_z.at[z], smz_s.at[k], smz_r.at[k], (lax.rem(z + 1 + k, nz) * 2 + x, g.t)
        )

    loop(nz - 1, lambda k: zsmall(k).start())
    loop(max(0, second.services() - done), lambda n: second.service(done + n))
    loop(max(0, first.services() - used), lambda n: first.service(used + n))
    small_z[z] = smalls[3]

    def zgot(k):
        remote(
            smalls.at[3], small_z.at[lax.rem(z - 1 - k + nz, nz)], smz_s.at[k], smz_r.at[k], g.sibling
        ).wait_recv()

    loop(nz - 1, zgot)
    small_out[...] = jnp.zeros_like(small_out)

    def zadd(k):
        small_out[...] += small_z[k]

    loop(nz, zadd)
    loop(nz - 1, lambda k: zsmall(k).wait_send())
    sums.drain()
    first.drain()
    second.drain()


def back_call(
    state_all, attended, w_out, numer, denom, key_valid, query, key, value, gain, small, normed,
    w_query, w_key, w_value, tokens, grad_state, collective_id,
):
    dp_size = lax.axis_size("dp")
    nz = dp_size // 2
    own_rows, width = tokens.shape
    bucket, values = attended.shape
    feat_width = query.shape[1]
    all_width = values + 2 * feat_width
    rows = width // dp_size
    halves = max(1, rows // 128)
    rn = rows // halves
    steps = halves * nz
    zslots = halves * (nz + 1)
    ahead = min(8, steps)
    ring = WeightSums.zs_slots(nz)
    vm, hbm = pl.BlockSpec(memory_space=pltpu.VMEM), pl.BlockSpec(memory_space=pl.ANY)
    dma = lambda *shape: pltpu.SemaphoreType.DMA(shape)
    vmem = lambda shape, kind=bf16: pltpu.VMEM(shape, kind)
    sds = jax.ShapeDtypeStruct

    def buffers(w):
        return [
            vmem((ahead, rn, w)), vmem((ring, rn, w)), vmem((2, rn, w), f32), vmem((rn, w)), vmem((rn, w)),
        ]

    def engine_sems():
        return [dma(ahead), dma(steps), dma(ring), dma(zslots), dma(3)]

    outs = pl.pallas_call(
        functools.partial(back_kernel, dp_size),
        out_shape=[
            sds((8, width), f32),
            sds((own_rows, width), f32),
            sds((1, values, rows), f32),
            sds((rows, values), f32),
            sds((1, 2 * feat_width, rows), f32),
            sds((steps, rn, values), bf16),
            sds((zslots, rn, values), bf16),
            sds((steps, rn, all_width), bf16),
            sds((zslots, rn, all_width), bf16),
        ],
        in_specs=[vm] * 11 + [hbm] * 6,
        out_specs=[vm] + [hbm] * 8,
        scratch_shapes=[
            vmem((1, bucket, width)), vmem((feat_width, width)), vmem((feat_width, width)), vmem((width, values)),
            vmem((own_rows, width)), vmem((own_rows, width), f32), vmem((bucket, values)), vmem((8, bucket), f32),
            vmem((feat_width, bucket)), vmem((1, bucket, all_width)),
            vmem((bucket, values), f32), vmem((bucket, feat_width), f32), vmem((feat_width, bucket), f32),
            vmem((2, own_rows, width)), vmem((2, own_rows, width)), vmem((own_rows, width)), vmem((own_rows, width)),
            vmem((own_rows, width), f32),
            *buffers(values), *buffers(all_width), vmem((512, rn), f32), vmem((1, width), f32),
            vmem((4, 8, width), f32), vmem((3, 8, width), f32), vmem((nz, 8, width), f32),
            dma(6), dma(1, 2, 4), dma(1, 2, 4), dma(1, 4), dma(1, 4),
            *engine_sems(), *engine_sems(), dma(3), dma(3), dma(nz), dma(nz),
        ],
        compiler_params=pltpu.CompilerParams(
            collective_id=collective_id, has_side_effects=True, vmem_limit_bytes=60 << 20
        ),
        name="attention_back",
    )(
        state_all[None], attended[None], w_out, numer, denom, key_valid, query, key, value, gain, small,
        normed, w_query, w_key, w_value, tokens, grad_state,
    )
    return outs[:5]


def per_device(
    tokens,
    gain_attn,
    gain_mlp,
    w_query,
    w_key,
    w_value,
    w_out,
    w_gate,
    w_up,
    w_down,
    cotangent,
    lengths,
):
    tok_rows = tokens.shape[0]
    groups = lax.axis_size("tensor")
    bucket = tok_rows * groups
    length = lengths[lax.axis_index("dp")]
    position = jnp.arange(bucket, dtype=jnp.int32)
    valid_rows = (position < length).astype(jnp.float32)
    own_rows = lax.axis_index("tensor") * tok_rows + jnp.arange(tok_rows, dtype=jnp.int32)
    own_valid = (own_rows < length).astype(jnp.float32)[:, None]
    head_count = w_query.shape[1] // FEAT
    head_width = w_value.shape[1] // head_count
    qk_scale = 1.0 / math.sqrt(FEAT)
    block_rows = min(512, bucket)
    float_single = jnp.float32
    bf16 = jnp.bfloat16
    x_full = tokens.astype(float_single)
    normed = (norm_parts(x_full)[0] * gain_attn).astype(bf16)
    normed_all = lax.all_gather(normed, "tensor", axis=0, tiled=True)
    query_rows = (
        jnp.dot(normed_all, w_query, preferred_element_type=float_single)
        .astype(bf16)
        .reshape(bucket, head_count, FEAT)
    )
    key_head_rows = (
        jnp.dot(normed_all, w_key, preferred_element_type=float_single)
        .astype(bf16)
        .reshape(bucket, head_count, FEAT)
    )
    value_heads = (
        jnp.dot(normed_all, w_value, preferred_element_type=float_single)
        .astype(bf16)
        .reshape(bucket, head_count, head_width)
    )

    def block_scores(first_row_index, last_row_index):
        scores = (
            jnp.einsum(
                "wra,tra->rwt",
                query_rows[first_row_index:last_row_index],
                key_head_rows[:last_row_index],
                preferred_element_type=float_single,
            )
            * qk_scale
        )
        key_mask = (
            (position[None, :last_row_index] <= position[first_row_index:last_row_index, None])
            & (position[None, :last_row_index] < length)
        ).astype(float_single)
        taylor = (1.0 + scores + 0.5 * scores * scores) * key_mask
        return (scores, key_mask, taylor)

    numer_parts = []
    denom_parts = []
    for first_row_index in range(0, bucket, block_rows):
        last_row_index = first_row_index + block_rows
        scores, key_mask, taylor = block_scores(first_row_index, last_row_index)
        numer_parts.append(
            jnp.einsum(
                "hqk,khv->qhv",
                taylor.astype(bf16),
                value_heads[:last_row_index],
                preferred_element_type=float_single,
            )
        )
        denom_parts.append(jnp.sum(taylor, axis=-1).T)
    numerator = jnp.concatenate(numer_parts, axis=0)
    denominator = jnp.concatenate(denom_parts, axis=0)
    attended = (
        (numerator / denominator[:, :, None]).reshape(bucket, head_count * head_width).astype(bf16)
    )
    den_part = jnp.sum(denominator * (valid_rows / (position + 1.0))[:, None])
    grad_out = cotangent.astype(float_single) * own_valid
    grad_mlp_all = lax.all_gather(grad_out.astype(bf16), "tensor", axis=0, tiled=True)
    output, grad_state, gain_mlp_part, grad_attn_all, mlp_totals = mlp_call(
        attended, w_out, tokens, gain_mlp[None], own_valid, w_gate.T, w_up.T, w_down, grad_mlp_all, 1
    )
    small = jnp.concatenate(
        [
            jnp.zeros_like(gain_mlp_part),
            gain_mlp_part,
            jnp.broadcast_to(den_part, (6, gain_mlp_part.shape[1])),
        ],
        axis=0,
    )
    key_valid = valid_rows[:, None]
    small_total, input_grad, out_total, value_total, qk_total = back_call(
        grad_attn_all,
        attended,
        w_out,
        numerator.reshape(bucket, head_count * head_width),
        denominator,
        key_valid,
        query_rows.reshape(bucket, head_count * FEAT),
        key_head_rows.reshape(bucket, head_count * FEAT),
        value_heads.reshape(bucket, head_count * head_width),
        gain_attn[None],
        small,
        normed_all,
        w_query.T,
        w_key.T,
        w_value,
        tokens,
        grad_state,
        2,
    )
    gain_attn_total, gain_mlp_total, den_total = small_total[0], small_total[1], small_total[2, 0]
    query_total = qk_total[0, : head_count * FEAT].T
    key_total = qk_total[0, head_count * FEAT :].T
    out_total = out_total[0]
    down_total, gate_total, up_total = mlp_totals[0], mlp_totals[1].T, mlp_totals[2].T
    den_mean = den_total / (head_count * groups * jnp.sum(lengths).astype(float_single))
    return (
        output,
        input_grad,
        gain_attn_total,
        gain_mlp_total,
        query_total,
        key_total,
        value_total,
        out_total,
        gate_total,
        up_total,
        down_total,
        den_mean,
    )


def solution(mesh):
    return jax.shard_map(
        per_device,
        mesh=mesh,
        in_specs=(
            P(("dp", "tensor"), None),
            P(),
            P(),
            P(None, "tensor"),
            P(None, "tensor"),
            P(None, "tensor"),
            P("tensor", None),
            P(None, "tensor"),
            P(None, "tensor"),
            P("tensor", None),
            P(("dp", "tensor"), None),
            P(),
        ),
        out_specs=(
            P(("dp", "tensor"), None),
            P(("dp", "tensor"), None),
            P(),
            P(),
            P("dp", "tensor"),
            P("dp", "tensor"),
            P("dp", "tensor"),
            P("tensor", "dp"),
            P("dp", "tensor"),
            P("dp", "tensor"),
            P("tensor", "dp"),
            P(),
        ),
        check_vma=False,
    )
```

profile of v0, /device:TPU:0, one launch (start us, length us, event | category | flops | bytes accessed | tf_op | source)
XLA Modules:
  0.0 484.4 jit_solution(11765169081105667524)
XLA Ops:
  7.2 1.6 fusion.6
  8.8 2.5 fusion.8
  12.7 1.2 multiply_convert_fusion
  16.6 1.3 fusion.16.valid
  17.9 1.5 fusion.15.key_valid
  21.2 1.7 fusion.14
  22.9 25.8 %all-gather.3.cloned.1.call-done.normed_h = bf16[1024,2048]{1,0:T(8,128)(2,1)} async-done(((bf16[256,2048]{1,0:T(8,128)(2,1)}), bf16[1024,2048]{1,0:T(8,128)(2,1)}) %all-gather.3.cloned.1.call-update) | async-done | bytes 4194320 | tf_op jit(solution)/shard_map/all_gather | solution.py:1017
  48.7 3.6 convolution_convert_fusion.2
  53.1 4.5 convolution_convert_fusion.value
  57.7 1.5 copy.92
  59.2 4.0 convolution_convert_fusion.1.query
  64.4 1.3 fusion.4
  67.0 1.3 copy.91
  68.3 1.3 copy.94
  69.6 4.6 fusion
  75.8 5.7 %fusion.2 = f32[4,128,512]{2,1,0:T(8,128)S(1)} fusion(bf16[1024,4,128]{0,2,1:T(8,128)(2,1)} %bitcast.79, f32[4,512,1024]{2,1,0:T(8,128)} %get-tuple-element.44, f32[512,1024]{1,0:T(8,128)} %fusion.14), kind=kOutput, calls=%fused_computation.4 | convolution fusion | flops 551550976 | bytes 12582912 | tf_op jit(solution)/shard_map/hqk,khv->qhv/dot_general | solution.py:1057
  81.5 1.5 pad_maximum_fusion
  83.0 2.9 copy.96.numer
  86.0 1.3 copy.93
  87.3 1.3 copy.95
  88.6 1.2 div.40
  89.8 1.8 div.43
  91.7 3.7 fusion.10.attended
  95.4 1.4 fusion.9.attended
  96.8 264.2 %mlp.1 = (bf16[256,2048]{1,0:T(8,128)(2,1)}, f32[256,2048]{1,0:T(8,128)}, f32[1,2048]{1,0:T(1,128)}, bf16[1024,2048]{1,0:T(8,128)(2,1)}, f32[3,1376,256]{2,1,0:T...) custom-call(bf16[1024,512]{1,0:T(8,128)(2,1)} %fusion.9.attended, ...), custom_call_target="tpu_custom_call" | custom-call | tf_op jit(solution)/shard_map/mlp/pallas_call | solution.py:686
  361.1 1.4 maximum_maximum_fusion.small_in
  362.5 100.4 %attention_back.1 = (f32[8,2048]{1,0:T(8,128)}, f32[256,2048]{1,0:T(8,128)}, f32[1,512,256]{2,1,0:T(8,128)}, f32[256,512]{1,0:T(8,128)}, f32[1,128,256]{2,1,0:T(...) custom-call(bf16[1,1024,2048]{2,1,0:T(8,128)(2,1)} %bitcast.77, ...), custom_call_target="tpu_custom_call" | custom-call | tf_op jit(solution)/shard_map/attention_back/pallas_call | solution.py:949
  462.9 1.2 slice.75
  464.1 1.5 fusion.24
  465.6 1.5 slice_bitcast_fusion.3
  467.1 4.5 slice_bitcast_fusion
  473.3 1.3 copy.104
  (72 shorter events, 12.7 us)
Async XLA Ops:
  7.2 4.3 copy-start.18
  7.2 5.5 %copy-start.12 = (bf16[256,2048]{1,0:T(8,128)(2,1)S(1)}, bf16[256,2048]{1,0:T(8,128)(2,1)}, u32[]{:S(2)}) copy-start(bf16[256,2048]{1,0:T(8,128)(2,1)} %param.22) | copy-start | bytes 3145732
  7.2 41.5 %all-gather.3.cloned.1.call-start = ((), (), s32[]{:S(2)}) async-start(), calls=%async_computation | async-start | bytes 5242880 | tf_op jit(solution)/shard_map/all_gather | solution.py:1017
  11.4 37.4 %copy-start.7 = (bf16[2048,64]{0,1:T(8,128)(2,1)S(1)}, bf16[2048,64]{0,1:T(8,128)(2,1)}, u32[]{:S(2)}) copy-start(bf16[2048,64]{0,1:T(8,128)(2,1)} %param.16) | copy-start | bytes 786436
  11.4 85.4 %all-gather.5.cloned.1.call-start = ((), (), s32[]{:S(2)}) async-start(), calls=%async_computation.1 | async-start | bytes 5242880 | tf_op jit(solution)/shard_map/all_gather | solution.py:1072
  21.2 31.9 %copy-start.4 = (bf16[2048,512]{1,0:T(8,128)(2,1)S(1)}, bf16[2048,512]{1,0:T(8,128)(2,1)}, u32[]{:S(2)}) copy-start(bf16[2048,512]{1,0:T(8,128)(2,1)} %w_value_h.1) | copy-start | bytes 6291460
  52.3 5.4 %copy-start.13 = (bf16[1024,64]{0,1:T(8,128)(2,1)}, bf16[1024,64]{0,1:T(8,128)(2,1)S(1)}, u32[]{:S(2)}) copy-start(bf16[1024,64]{0,1:T(8,128)(2,1)S(1)} %convolution_convert_fusion.2) | copy-start | bytes 393220
  57.7 5.5 %copy-start = (bf16[1024,512]{1,0:T(8,128)(2,1)}, bf16[1024,512]{1,0:T(8,128)(2,1)S(1)}, u32[]{:S(2)}) copy-start(bf16[1024,512]{1,0:T(8,128)(2,1)S(1)} %convolution_convert_fusion.value) | copy-start | bytes 3145732
  59.2 5.2 %copy-start.10 = (f32[512,512]{0,1:T(8,128)S(1)}, f32[512,512]{0,1:T(8,128)}, u32[]{:S(2)}) copy-start(f32[512,512]{0,1:T(8,128)} %and_convert_fusion) | copy-start | bytes 3145732
  59.2 5.2 %slice-start = ((bf16[1024,64]{0,1:T(8,128)(2,1)}), bf16[512,64]{0,1:T(8,128)(2,1)S(1)}, s32[]{:S(2)}) async-start(bf16[1024,64]{0,1:T(8,128)(2,1)} %copy-done.13), calls=%async_computation.2 | async-start | bytes 131072 | tf_op jit(solution)/shard_map/slice | solution.py:1039
  63.2 2.6 copy-start.8
  64.4 1.3 copy-start.11
  64.4 1.4 copy-start.17
  65.8 3.8 copy-start.5
  65.8 3.8 copy-start.14
  75.8 12.7 %copy-start.1 = (f32[1024,4]{1,0:T(8,128)}, f32[1024,4]{1,0:T(8,128)S(1)}, u32[]{:S(2)}) copy-start(f32[1024,4]{1,0:T(8,128)S(1)} %copy.80.denom) | copy-start | bytes 49156
  89.8 5.6 %copy-start.2 = (f32[512,512]{1,0:T(8,128)S(1)}, f32[512,512]{1,0:T(8,128)}, u32[]{:S(2)}) copy-start(f32[512,512]{1,0:T(8,128)} %copy.91) | copy-start | bytes 3145732
  91.7 3.7 copy-start.3
  467.1 5.1 %copy-start.9 = (bf16[256,2048]{1,0:T(8,128)(2,1)S(1)}, bf16[256,2048]{1,0:T(8,128)(2,1)}, u32[]{:S(2)}) copy-start(bf16[256,2048]{1,0:T(8,128)(2,1)} %get-tuple-element.59) | copy-start | bytes 3145732
  467.1 6.1 %copy-start.6 = (f32[256,2048]{1,0:T(8,128)S(1)}, f32[256,2048]{1,0:T(8,128)}, u32[]{:S(2)}) copy-start(f32[256,2048]{1,0:T(8,128)} %get-tuple-element.60) | copy-start | bytes 6291460
  472.2 2.3 copy-start.16
  472.3 3.1 copy-start.15
Sparse Core Ops, SparseCore 0:
  11.5 37.1 all-gather.2
  50.8 34.4 all-gather.4
where the time goes:
time: 491 us; the launch traced here: 484 us
  Pallas kernels  365 us (74%)
  local copies, waits for them, and re-layouts  29.1 us (6%)
  waiting for transfers between devices  25.8 us (5%)
  matrix products  24.8 us (5%)
  other arithmetic  22.9 us (5%)
  between operations  17.1 us (3%)
    pallas_call x1, Pallas kernels, mlp_call(): pl.pallas_call(functools.partial(mlp_kernel, dp_size), out_shape=[sds((ow...  264 us
    pallas_call x1, Pallas kernels, back_call(): pl.pallas_call(functools.partial(back_kernel, dp_size), out_shape=[sds((8...  100 us
    all_gather x1, waiting for transfers between devices, per_device(): normed_all = lax.all_gather(normed, 'tensor', axis=0, tiled=True)  25.8 us
  transfers between devices with their start and end apart: 2, of which 1 were waited for; matrix products, arithmetic and copies ran while one was open for 12% of the time, Pallas kernels for 0%

commit v1 on v0

--- a/solution.py
+++ b/solution.py
@@ -401,6 +401,12 @@
 
 
 def meet(g, nz, every=False):
+    if nz == 0:
+        barrier = pltpu.get_barrier_semaphore()
+        for device in (g.sibling, g.across):
+            pl.semaphore_signal(barrier, inc=1, device_id=device, device_id_type=MESH)
+        pl.semaphore_wait(barrier, 2)
+        return
     z, x = g.dp // 2, lax.rem(g.dp, 2)
     barrier = pltpu.get_barrier_semaphore()
 
@@ -427,16 +433,23 @@
     pl.semaphore_wait(barrier, peers)
 
 
-def turned(out, turn, sem, halves, rn):
+def turned(outs, turn, sem, halves, rn):
+    def put(out, n, w, h):
+        to = out.at[pl.ds(n, w)]
+        if halves > 1:
+            to = out.at[pl.ds(n, w), pl.ds(pl.multiple_of(h * rn, rn), rn)]
+        copy = pltpu.make_async_copy(turn.at[pl.ds(0, w)], to, sem)
+        copy.start()
+        copy.wait()
+
     def emit(i, h, value):
-        for n, w in pieces(out.shape[1], 512):
+        for n, w in pieces(outs[0].shape[0], 512):
             turn[:w] = value(n, w).T
-            to = out.at[i, pl.ds(n, w)]
-            if halves > 1:
-                to = out.at[i, pl.ds(n, w), pl.ds(pl.multiple_of(h * rn, rn), rn)]
-            copy = pltpu.make_async_copy(turn.at[pl.ds(0, w)], to, sem)
-            copy.start()
-            copy.wait()
+            if len(outs) == 1:
+                put(outs[0], n, w, h)
+                continue
+            for m, out in enumerate(outs):
+                pl.when(i == m)(functools.partial(put, out, n, w, h))
 
     return emit
 
@@ -463,8 +476,8 @@
 
 def mlp_kernel(
     dp_size,
-    attended, w_out, gain, valid, tokens_h, w_gate_h, w_up_h, w_down_h, cot_h,
-    output, state_grad_h, gain_grad, state_all_h, totals_h, xrecv, zrecv, frecv, fxrecv,
+    attended, w_out, gain, length, tokens_h, w_gate_h, w_up_h, w_down_h, cot_h,
+    output, state_grad_h, gain_grad, state_all_h, down_h, gate_h, up_h, xrecv, zrecv, frecv, fxrecv,
     w_gate, w_up, w_down, lefts, rights, mid, sibsend, sibrecv, ysend, yrecv, total, spread_buf,
     xs, zs, zf, zfx, acc, facc, xtmp, ztmp, turn,
     load_sem, sib_s, sib_r, y_s, y_r, ag_s, ag_r,
@@ -564,7 +577,7 @@
     engine = WeightSums(
         g, dp_size, rows, 3, 1, block_of(lefts, rights, lambda i: jnp.minimum(i, 1), rows, halves),
         (xs, zs, acc, xtmp, ztmp, xrecv, zrecv, zf, zfx, facc, frecv, fxrecv),
-        (xs_s, xr_s, zs_s, zr_s, loc, zf_s, zf_r, fx_s, fx_r), turned(totals_h, turn, loc.at[2], halves, rn),
+        (xs_s, xr_s, zs_s, zr_s, loc, zf_s, zf_r, fx_s, fx_r), turned((down_h, gate_h, up_h), turn, loc.at[2], halves, rn),
     )
     engine.begin()
 
@@ -658,7 +671,9 @@
     used = used + sums.count
 
     def last_state(r, summed):
-        output[r] = (valid[r] * (mid[r] + summed)).astype(bf16)
+        position = own_first + r.start + lax.broadcasted_iota(jnp.int32, (STRIP, 1), 0)
+        valid = (position < length[...]).astype(f32)
+        output[r] = (valid * (mid[r] + summed)).astype(bf16)
 
     loop(sums.count, lambda j: sums.finish(j, last_state))
     loop(engine.services() - used, lambda n: engine.service(used + n))
@@ -668,7 +683,7 @@
     engine.drain()
 
 
-def mlp_call(attended, w_out, tokens, gain, valid, w_gate, w_up, w_down, cot_all, collective_id):
+def mlp_call(attended, w_out, tokens, gain, length, w_gate, w_up, w_down, cot_all, collective_id):
     dp_size = lax.axis_size("dp")
     nz = dp_size // 2
     own_rows, width = tokens.shape
@@ -690,14 +705,14 @@
             sds((own_rows, width), f32),
             sds((1, width), f32),
             sds((bucket, width), bf16),
-            sds((3, units, rows), f32),
+            *[sds((units, rows), f32)] * 3,
             sds((steps, rn, units), bf16),
             sds((jobs * (nz + 1), rn, units), bf16),
             sds((nz + 1, 2 * rn, units), bf16),
             sds((rn, units), bf16),
         ],
         in_specs=[vm] * 4 + [hbm] * 5,
-        out_specs=[vm, hbm, vm] + [hbm] * 6,
+        out_specs=[vm, hbm, vm] + [hbm] * 8,
         scratch_shapes=[
             vmem((units, width)), vmem((units, width)), vmem((units, width)),
             vmem((2, bucket, width)), vmem((3, bucket, units)), vmem((own_rows, width), f32),
@@ -713,8 +728,8 @@
             collective_id=collective_id, has_side_effects=True, vmem_limit_bytes=62 << 20
         ),
         name="mlp",
-    )(attended, w_out, gain, valid, tokens, w_gate, w_up, w_down, cot_all)
-    return outs[:5]
+    )(attended, w_out, gain, length, tokens, w_gate, w_up, w_down, cot_all)
+    return outs[:7]
 
 
 def head_lanes(h, feat, width):
@@ -723,7 +738,7 @@
 
 def back_kernel(
     dp_size,
-    state_all, attended, w_out, numer, denom, key_valid, query, key, value, gain, small_in,
+    state_all, attended, w_out, numer, denom, length, query, key, value, gain, mlp_gain, den_row,
     normed_h, w_query_h, w_key_h, w_value_h, tokens_h, grad_state_h,
     small_out, input_grad_h, out_h, value_h, qk_h, xrecv_o, zrecv_o, xrecv_a, zrecv_a,
     normed, w_query, w_key, w_value, tokens, grad_state, grad_numer, grad_den, key_t, rights,
@@ -760,9 +775,9 @@
     first = WeightSums(
         g, dp_size, rows, 1, 0, block_of(state_all, attended, lambda i: i, rows, halves),
         (xs_o, zs_o, acc_o, xtmp_o, ztmp_o, xrecv_o, zrecv_o),
-        (xs_so, xr_so, zs_so, zr_so, loc_o), turned(out_h, turn, loc_o.at[2], halves, rn),
+        (xs_so, xr_so, zs_so, zr_so, loc_o), turned((out_h,), turn, loc_o.at[2], halves, rn),
     )
-    turn_qk = turned(qk_h, turn, loc_a.at[2], halves, rn)
+    turn_qk = turned((qk_h,), turn, loc_a.at[2], halves, rn)
 
     def emit_attn(i, h, take):
         values = heads * head_width
@@ -814,7 +829,8 @@
             below = lax.broadcasted_iota(jnp.int32, (nk, tile), 0) <= q0 + lax.broadcasted_iota(
                 jnp.int32, (nk, tile), 1
             )
-            mask = below.astype(f32) * key_valid[:nk]
+            real = lax.broadcasted_iota(jnp.int32, (nk, 1), 0) < length[...]
+            mask = below.astype(f32) * real.astype(f32)
             taylor = (1.0 + scores + 0.5 * scores * scores) * mask
             grads = grad_numer[q0:nk, cols]
             gv_acc[:nk, cols] += dot(taylor.astype(bf16), grads)
@@ -876,8 +892,10 @@
     loop(sums.count, close)
     done = 3 * sums.count
 
-    smalls[0] = small_in[...]
+    smalls[0] = jnp.zeros(smalls.shape[1:], f32)
     smalls[0, 0:1] = gain_acc[...]
+    smalls[0, 1:2] = mlp_gain[...]
+    smalls[0, 2:3, : den_row.shape[1]] = den_row[...]
     z, x = second.z, second.x
     peers = (g.sibling, g.across, second.partner)
     for n, device in enumerate(peers):
@@ -917,7 +935,7 @@
 
 
 def back_call(
-    state_all, attended, w_out, numer, denom, key_valid, query, key, value, gain, small, normed,
+    state_all, attended, w_out, numer, denom, length, query, key, value, gain, mlp_gain, den_row, normed,
     w_query, w_key, w_value, tokens, grad_state, collective_id,
 ):
     dp_size = lax.axis_size("dp")
@@ -951,15 +969,15 @@
         out_shape=[
             sds((8, width), f32),
             sds((own_rows, width), f32),
-            sds((1, values, rows), f32),
+            sds((values, rows), f32),
             sds((rows, values), f32),
-            sds((1, 2 * feat_width, rows), f32),
+            sds((2 * feat_width, rows), f32),
             sds((steps, rn, values), bf16),
             sds((zslots, rn, values), bf16),
             sds((steps, rn, all_width), bf16),
             sds((zslots, rn, all_width), bf16),
         ],
-        in_specs=[vm] * 11 + [hbm] * 6,
+        in_specs=[vm] * 12 + [hbm] * 6,
         out_specs=[vm] + [hbm] * 8,
         scratch_shapes=[
             vmem((1, bucket, width)), vmem((feat_width, width)), vmem((feat_width, width)), vmem((width, values)),
@@ -978,10 +996,137 @@
         ),
         name="attention_back",
     )(
-        state_all[None], attended[None], w_out, numer, denom, key_valid, query, key, value, gain, small,
+        state_all[None], attended[None], w_out, numer, denom, length, query, key, value, gain, mlp_gain, den_row,
         normed, w_query, w_key, w_value, tokens, grad_state,
     )
     return outs[:5]
+
+
+def front_kernel(
+    tokens, cotangent, gain, length, w_query, w_key, w_value,
+    query, key, value, numer, attended, denom, den_row, normed_h, cot_h,
+    normed, cot_own, load_sem, ag_s, ag_r,
+):
+    g = Group()
+    own_rows = tokens.shape[0]
+    bucket = normed.shape[0]
+    feat_width = query.shape[1]
+    head_width = 128
+    heads = value.shape[1] // head_width
+    feat = feat_width // heads
+    scale = 1.0 / math.sqrt(feat)
+    own_first = pl.multiple_of(g.t * own_rows, own_rows)
+    meet(g, 0)
+    rows_out = Spread(g, own_rows, 64, None, normed, (ag_s, ag_r), 0)
+    cots = Spread(g, own_rows, 64, cot_own, cot_h, (ag_s, ag_r), 1)
+
+    def first_norm(j):
+        for a in range(64 // STRIP):
+            r = pl.ds(pl.multiple_of(j * 64 + a * STRIP, STRIP), STRIP)
+            to = pl.ds(pl.multiple_of(own_first + j * 64 + a * STRIP, STRIP), STRIP)
+            normal, _ = norm_parts(tokens[r].astype(f32))
+            normed[to] = (normal * gain[...]).astype(bf16)
+        rows_out.start(j)
+
+    loop(rows_out.count, first_norm)
+    position = own_first + lax.broadcasted_iota(jnp.int32, (own_rows, 1), 0)
+    real_rows = (position < length[...]).astype(f32)
+    cot_own[...] = (cotangent[...].astype(f32) * real_rows).astype(bf16)
+    own_cot = pltpu.make_async_copy(cot_own, cot_h.at[pl.ds(own_first, own_rows)], load_sem.at[0])
+    own_cot.start()
+
+    def project(y, c, half):
+        r = pl.ds(pl.multiple_of((y * 2 + c) * own_rows + half * 128, 128), 128)
+        value[r] = dot(normed[r], w_value[...]).astype(bf16)
+        query[r] = dot(normed[r], w_query[...], NT).astype(bf16)
+        key[r] = dot(normed[r], w_key[...], NT).astype(bf16)
+
+    def near(half):
+        project(g.y, g.c, half)
+        loop(2, lambda a: rows_out.sib_in(half * 2 + a))
+        project(g.y, 1 - g.c, half)
+
+    loop(2, near)
+
+    def far(half):
+        loop(2, lambda a: rows_out.relay(half * 2 + a))
+        project(1 - g.y, g.c, half)
+        loop(2, lambda a: rows_out.far_in(half * 2 + a))
+        project(1 - g.y, 1 - g.c, half)
+
+    loop(1, far)
+    loop(2, lambda a: rows_out.relay(2 + a))
+    loop(cots.count, cots.start)
+    project(1 - g.y, g.c, 1)
+    loop(2, lambda a: rows_out.far_in(2 + a))
+    project(1 - g.y, 1 - g.c, 1)
+    keep = pltpu.make_async_copy(normed, normed_h, load_sem.at[1])
+    keep.start()
+    denom[...] = jnp.zeros_like(denom)
+    tile = 256
+
+    def head(h):
+        lanes = head_lanes(h, feat, feat_width)
+        cols = pl.ds(pl.multiple_of(h * head_width, head_width), head_width)
+        for qb in range(bucket // tile):
+            q0, nk = qb * tile, (qb + 1) * tile
+            scores = dot(query[q0:nk] * lanes, key[:nk], NT) * scale
+            spot = lax.broadcasted_iota(jnp.int32, (tile, nk), 1)
+            below = spot <= q0 + lax.broadcasted_iota(jnp.int32, (tile, nk), 0)
+            real = lax.broadcasted_iota(jnp.int32, (1, nk), 1) < length[...]
+            taylor = (1.0 + scores + 0.5 * scores * scores) * (below.astype(f32) * real.astype(f32))
+            den = jnp.sum(taylor, axis=1, keepdims=True)
+            top = dot(taylor.astype(bf16), value[:nk, cols])
+            numer[q0:nk, cols] = top
+            attended[q0:nk, cols] = (top / den).astype(bf16)
+            lane = lax.broadcasted_iota(jnp.int32, (tile, denom.shape[1]), 1)
+            denom[q0:nk] = jnp.where(lane == h, den, denom[q0:nk])
+
+    for h in range(heads):
+        head(h)
+        if h < cots.count:
+            cots.relay(h)
+    for h in range(heads, cots.count):
+        cots.relay(h)
+    place = lax.broadcasted_iota(jnp.int32, (bucket, 1), 0)
+    weight = (place < length[...]).astype(f32) / (place.astype(f32) + 1.0)
+    den_row[...] = jnp.sum(denom[...] * weight, axis=0, keepdims=True)
+
+    def arrive(j):
+        cots.sib_in(j)
+        cots.far_in(j)
+
+    loop(cots.count, arrive)
+    own_cot.wait()
+    keep.wait()
+    rows_out.drain()
+    cots.drain()
+
+
+def front_call(tokens, cotangent, gain, length, w_query, w_key, w_value, collective_id):
+    own_rows, width = tokens.shape
+    bucket = own_rows * lax.axis_size("tensor")
+    feat_width, values = w_query.shape[0], w_value.shape[1]
+    vm, hbm = pl.BlockSpec(memory_space=pltpu.VMEM), pl.BlockSpec(memory_space=pl.ANY)
+    dma = lambda *shape: pltpu.SemaphoreType.DMA(shape)
+    sds = jax.ShapeDtypeStruct
+    return pl.pallas_call(
+        front_kernel,
+        out_shape=[
+            sds((bucket, feat_width), bf16), sds((bucket, feat_width), bf16), sds((bucket, values), bf16),
+            sds((bucket, values), f32), sds((bucket, values), bf16), sds((bucket, 128), f32), sds((1, 128), f32),
+            sds((bucket, width), bf16), sds((bucket, width), bf16),
+        ],
+        in_specs=[vm] * 7,
+        out_specs=[vm] * 7 + [hbm] * 2,
+        scratch_shapes=[
+            pltpu.VMEM((bucket, width), bf16), pltpu.VMEM((own_rows, width), bf16), dma(2), dma(2, 3, 4), dma(2, 3, 4),
+        ],
+        compiler_params=pltpu.CompilerParams(
+            collective_id=collective_id, has_side_effects=True, vmem_limit_bytes=48 << 20
+        ),
+        name="front",
+    )(tokens, cotangent, gain, length, w_query, w_key, w_value)
 
 
 def per_device(
@@ -998,116 +1143,25 @@
     cotangent,
     lengths,
 ):
-    tok_rows = tokens.shape[0]
     groups = lax.axis_size("tensor")
-    bucket = tok_rows * groups
-    length = lengths[lax.axis_index("dp")]
-    position = jnp.arange(bucket, dtype=jnp.int32)
-    valid_rows = (position < length).astype(jnp.float32)
-    own_rows = lax.axis_index("tensor") * tok_rows + jnp.arange(tok_rows, dtype=jnp.int32)
-    own_valid = (own_rows < length).astype(jnp.float32)[:, None]
-    head_count = w_query.shape[1] // FEAT
-    head_width = w_value.shape[1] // head_count
-    qk_scale = 1.0 / math.sqrt(FEAT)
-    block_rows = min(512, bucket)
-    float_single = jnp.float32
-    bf16 = jnp.bfloat16
-    x_full = tokens.astype(float_single)
-    normed = (norm_parts(x_full)[0] * gain_attn).astype(bf16)
-    normed_all = lax.all_gather(normed, "tensor", axis=0, tiled=True)
-    query_rows = (
-        jnp.dot(normed_all, w_query, preferred_element_type=float_single)
-        .astype(bf16)
-        .reshape(bucket, head_count, FEAT)
+    length = lax.dynamic_slice(lengths, (lax.axis_index("dp"),), (1,))[None]
+    w_query_t, w_key_t, w_gate_t, w_up_t = w_query.T, w_key.T, w_gate.T, w_up.T
+    query, key, value, numer, attended, denom, den_row, normed_all, cot_all = front_call(
+        tokens, cotangent, gain_attn[None], length, w_query_t, w_key_t, w_value, 3
     )
-    key_head_rows = (
-        jnp.dot(normed_all, w_key, preferred_element_type=float_single)
-        .astype(bf16)
-        .reshape(bucket, head_count, FEAT)
+    output, grad_state, mlp_gain, state_all, down_total, gate_total, up_total = mlp_call(
+        attended, w_out, tokens, gain_mlp[None], length, w_gate_t, w_up_t, w_down, cot_all, 1
     )
-    value_heads = (
-        jnp.dot(normed_all, w_value, preferred_element_type=float_single)
-        .astype(bf16)
-        .reshape(bucket, head_count, head_width)
+    small, input_grad, out_total, value_total, qk_total = back_call(
+        state_all, attended, w_out, numer, denom, length, query, key, value, gain_attn[None], mlp_gain, den_row,
+        normed_all, w_query_t, w_key_t, w_value, tokens, grad_state, 2,
     )
-
-    def block_scores(first_row_index, last_row_index):
-        scores = (
-            jnp.einsum(
-                "wra,tra->rwt",
-                query_rows[first_row_index:last_row_index],
-                key_head_rows[:last_row_index],
-                preferred_element_type=float_single,
-            )
-            * qk_scale
-        )
-        key_mask = (
-            (position[None, :last_row_index] <= position[first_row_index:last_row_index, None])
-            & (position[None, :last_row_index] < length)
-        ).astype(float_single)
-        taylor = (1.0 + scores + 0.5 * scores * scores) * key_mask
-        return (scores, key_mask, taylor)
-
-    numer_parts = []
-    denom_parts = []
-    for first_row_index in range(0, bucket, block_rows):
-        last_row_index = first_row_index + block_rows
-        scores, key_mask, taylor = block_scores(first_row_index, last_row_index)
-        numer_parts.append(
-            jnp.einsum(
-                "hqk,khv->qhv",
-                taylor.astype(bf16),
-                value_heads[:last_row_index],
-                preferred_element_type=float_single,
-            )
-        )
-        denom_parts.append(jnp.sum(taylor, axis=-1).T)
-    numerator = jnp.concatenate(numer_parts, axis=0)
-    denominator = jnp.concatenate(denom_parts, axis=0)
-    attended = (
-        (numerator / denominator[:, :, None]).reshape(bucket, head_count * head_width).astype(bf16)
-    )
-    den_part = jnp.sum(denominator * (valid_rows / (position + 1.0))[:, None])
-    grad_out = cotangent.astype(float_single) * own_valid
-    grad_mlp_all = lax.all_gather(grad_out.astype(bf16), "tensor", axis=0, tiled=True)
-    output, grad_state, gain_mlp_part, grad_attn_all, mlp_totals = mlp_call(
-        attended, w_out, tokens, gain_mlp[None], own_valid, w_gate.T, w_up.T, w_down, grad_mlp_all, 1
-    )
-    small = jnp.concatenate(
-        [
-            jnp.zeros_like(gain_mlp_part),
-            gain_mlp_part,
-            jnp.broadcast_to(den_part, (6, gain_mlp_part.shape[1])),
-        ],
-        axis=0,
-    )
-    key_valid = valid_rows[:, None]
-    small_total, input_grad, out_total, value_total, qk_total = back_call(
-        grad_attn_all,
-        attended,
-        w_out,
-        numerator.reshape(bucket, head_count * head_width),
-        denominator,
-        key_valid,
-        query_rows.reshape(bucket, head_count * FEAT),
-        key_head_rows.reshape(bucket, head_count * FEAT),
-        value_heads.reshape(bucket, head_count * head_width),
-        gain_attn[None],
-        small,
-        normed_all,
-        w_query.T,
-        w_key.T,
-        w_value,
-        tokens,
-        grad_state,
-        2,
-    )
-    gain_attn_total, gain_mlp_total, den_total = small_total[0], small_total[1], small_total[2, 0]
-    query_total = qk_total[0, : head_count * FEAT].T
-    key_total = qk_total[0, head_count * FEAT :].T
-    out_total = out_total[0]
-    down_total, gate_total, up_total = mlp_totals[0], mlp_totals[1].T, mlp_totals[2].T
-    den_mean = den_total / (head_count * groups * jnp.sum(lengths).astype(float_single))
+    gain_attn_total, gain_mlp_total = small[0], small[1]
+    feat_width = w_query.shape[1]
+    query_total, key_total = qk_total[:feat_width].T, qk_total[feat_width:].T
+    gate_total, up_total = gate_total.T, up_total.T
+    heads = feat_width // FEAT * groups
+    den_mean = jnp.sum(small[2, :128]) / (heads * jnp.sum(lengths).astype(f32))
     return (
         output,
         input_grad,

time: 491 us -> 459 us (0.935)
  Pallas kernels: 365 us -> 422 us
  waiting for transfers between devices: 25.8 us -> 0 us
  matrix products: 24.8 us -> 0 us
  other arithmetic: 22.9 us -> 1.91 us
  between operations: 17.1 us -> 3.61 us
  local copies, waits for them, and re-layouts: 29.1 us -> 22.1 us
    pallas_call x0 -> x1, Pallas kernels: none -> 55.9 us  [front_call(): pl.pallas_call(front_kernel, out_shape=[sds((bucket, feat_width), bf16),...]
    all_gather x2 -> x0, waiting for transfers between devices: 25.8 us -> none  [the longest x1 25.8 us: per_device(): normed_all = lax.all_gather(normed, 'tensor', axis=0, tiled=True)]
    dot_general x7 -> x0, matrix products: 24.8 us -> none  [the longest x2 6.84 us: per_device(): jnp.einsum('hqk,khv->qhv', taylor.astype(bf16), value_heads[:last_row_ind...]
    convert_element_type x9 -> x0, other arithmetic: 15.2 us -> none  [the longest x2 5.15 us: per_device(): (numerator / denominator[:, :, None]).reshape(bucket, head_count * head_w...]
    unnamed x42 -> x45, local copies, waits for them, and re-layouts: 4.03 us -> 17.7 us
    concatenate x7 -> x0, local copies, waits for them, and re-layouts: 5.52 us -> none  [the longest x4 5.23 us: per_device(): numerator = jnp.concatenate(numer_parts, axis=0)]
  transfers between devices with their start and end apart: 2 -> 0, of which waited for: 1 -> 0; matrix products, arithmetic and copies ran while one was open for 12% -> 0% of each run, Pallas kernels for 0% -> 0%
where the time goes in v1:
time: 459 us; the launch traced here: 450 us
  Pallas kernels  422 us (92%)
  local copies, waits for them, and re-layouts  22.1 us (5%)
    pallas_call x1, Pallas kernels, mlp_call(): pl.pallas_call(functools.partial(mlp_kernel, dp_size), out_shape=[sds((ow...  265 us
    pallas_call x1, Pallas kernels, back_call(): pl.pallas_call(functools.partial(back_kernel, dp_size), out_shape=[sds((8...  101 us
    pallas_call x1, Pallas kernels, front_call(): pl.pallas_call(front_kernel, out_shape=[sds((bucket, feat_width), bf16),...  55.9 us
    unnamed x45, local copies, waits for them, and re-layouts  17.7 us

profile of v1, /device:TPU:0, one launch (start us, length us, event | category | flops | bytes accessed | tf_op | source)
XLA Modules:
  0.0 449.9 jit_solution(13455192387448803978)
XLA Ops:
  0.6 1.2 dynamic_slice.3
  1.9 1.2 copy-done
  3.1 0.9 copy-done.2
  4.1 0.9 copy-done.3
  5.0 1.2 copy-done.4
  6.2 0.7 copy-done.9
  6.9 55.9 %front.1 = (bf16[1024,64]{1,0:T(8,128)(2,1)S(1)}, bf16[1024,64]{1,0:T(8,128)(2,1)S(1)}, bf16[1024,512]{1,0:T(8,128)(2,1)S(1)}, f32[1024,512]{1,0:T(8,128)}, bf16...) custom-call(bf16[256,2048]{1,0:T(8,128)(2,1)S(1)} %copy-done, ...), custom_call_target="tpu_custom_call" | custom-call | tf_op jit(solution)/shard_map/front/pallas_call | solution.py:1113
  62.9 0.0 copy-start.1
  62.9 1.0 copy-done.1
  63.9 1.0 copy-done.5
  64.8 0.8 copy-done.6
  65.6 0.7 copy-done.7
  66.3 0.7 copy-done.8
  67.0 0.5 copy-done.10
  67.5 265.3 %mlp.1 = (bf16[256,2048]{1,0:T(8,128)(2,1)}, f32[256,2048]{1,0:T(8,128)}, f32[1,2048]{1,0:T(1,128)}, bf16[1024,2048]{1,0:T(8,128)(2,1)}, f32[1376,256]{1,0:T(8,1...) custom-call(bf16[1024,512]{1,0:T(8,128)(2,1)} %copy-done.1, ...), custom_call_target="tpu_custom_call" | custom-call | tf_op jit(solution)/shard_map/mlp/pallas_call | solution.py:701
  332.8 0.0 copy-start.18
  332.8 0.0 copy-start.15
  332.8 101.0 %attention_back.1 = (f32[8,2048]{1,0:T(8,128)}, f32[256,2048]{1,0:T(8,128)}, f32[512,256]{1,0:T(8,128)}, f32[256,512]{1,0:T(8,128)}, f32[128,256]{1,0:T(8,128)},...) custom-call(bf16[1,1024,2048]{2,1,0:T(8,128)(2,1)} %bitcast.26, ...), custom_call_target="tpu_custom_call" | custom-call | tf_op jit(solution)/shard_map/attention_back/pallas_call | solution.py:967
  433.9 1.7 slice_bitcast_fusion
  435.6 1.5 fusion
  437.1 1.3 slice_reduce_fusion
  438.4 0.0 copy-done.18
  438.4 0.6 reduce_sum.19
  440.3 1.0 copy.31
  441.3 1.3 copy.32
  442.6 0.0 copy-done.17
  442.7 0.8 copy.33
  443.5 0.8 copy.34
  444.3 1.1 copy.35
  445.4 1.1 copy.36
  446.5 0.8 copy-done.12
  447.2 1.1 copy.37
  (21 shorter events, 0.0 us)
Async XLA Ops:
  1.9 1.2 copy-start
  3.1 0.9 copy-start.2
  4.1 0.9 copy-start.3
  5.0 1.2 copy-start.4
  6.2 0.7 copy-start.9
  62.9 1.0 copy-start.1
  63.9 1.0 copy-start.5
  64.8 0.8 copy-start.6
  65.6 0.7 copy-start.7
  66.3 0.7 copy-start.8
  67.0 0.5 copy-start.10
  332.8 105.6 %copy-start.18 = (s32[8]{0:T(128)S(1)}, s32[8]{0:T(128)}, u32[]{:S(2)}) copy-start(s32[8]{0:T(128)} %param.23) | copy-start | bytes 100
  332.8 107.5 %copy-start.15 = (bf16[256,2048]{1,0:T(8,128)(2,1)S(1)}, bf16[256,2048]{1,0:T(8,128)(2,1)}, u32[]{:S(2)}) copy-start(bf16[256,2048]{1,0:T(8,128)(2,1)} %get-tuple-element.70) | copy-start | bytes 3145732
  433.9 7.4 %copy-start.11 = (f32[256,2048]{1,0:T(8,128)S(1)}, f32[256,2048]{1,0:T(8,128)}, u32[]{:S(2)}) copy-start(f32[256,2048]{1,0:T(8,128)} %get-tuple-element.71) | copy-start | bytes 6291460
  441.3 1.4 copy-start.17
  441.3 2.2 copy-start.16
  441.3 3.0 copy-start.14
  443.5 1.9 copy-start.13
  445.4 1.9 copy-start.12
